TPU v7x, 32 devices: a whole 2x2x4 slice. The times are simulated.
32 devices in a mesh: mem: 4 (over y, x), patch: 8 (over z, core).
Axes of the slice: x: 2, y: 2, z: 4, core: 2. Of those that a mesh axis runs over, the one named last changes fastest.
Arguments:
- prior: bfloat16 [80, 32, 32768], P('mem', 'patch'), may hold values from -6 to 6
- obs_prior: bfloat16 [4096, 80, 128], P(('mem', 'patch')), may hold values from -8 to 8
- obs_depart: bfloat16 [4096, 128], P(('mem', 'patch')), may hold values from -6 to 6
- obs_rinv: bfloat16 [4096, 128], P(('mem', 'patch')), may hold values from 0.25 to 2
- loc_class: int32 [4096, 128], P(('mem', 'patch')), may hold values from 0 to 15
- block_owner: int32 [4096, 1], P(('mem', 'patch')), may hold values from 0 to 31; in each aligned block of 128 rows (0 to 127, 128 to 255, ...) at most 8 rows name the same one
- block_patch: int32 [4096], P(('mem', 'patch')), may hold values from 0 to 15
Outputs:
- analysis: bfloat16 [80, 32, 32768], P('mem', 'patch')
Inputs may be any that keep to these rules, and one draw needn't show every extreme that they name: `block_owner`: in each aligned block of 128 rows (the rows of one device) no device index appears more than 8 times, a bound that some block reaches.
All inputs are finite; a program needn't handle non-finite values.
Results may differ from a plain program's by a relative error of at most 0.012.
Values may be sent and summed in bfloat16 or wider, within the bound.
A program may use at most 384 MiB of HBM per device.

v0:
```python
import jax
import jax.numpy as jnp
from jax import lax
from jax.sharding import PartitionSpec as P

PD = 16
ITERS = 10


def loc_weight(classes):
    taper = 1.0 - classes.astype(jnp.float32) * 0.0625
    return taper * taper


def block_terms(values, depart, rinv, classes):
    average = jnp.sum(values, axis=1, keepdims=True, dtype=jnp.float32) / values.shape[1]
    deviation = (values.astype(jnp.float32) - average).astype(jnp.bfloat16)
    factor = loc_weight(classes) * rinv.astype(jnp.float32)
    scaled = (deviation.astype(jnp.float32) * factor[:, None, :]).astype(jnp.bfloat16)
    gram_blocks = jnp.einsum("bko,bjo->bkj", scaled, deviation, preferred_element_type=jnp.float32)
    drive_vec = jnp.einsum("bko,bo->bk", scaled, depart, preferred_element_type=jnp.float32)
    return (gram_blocks, drive_vec)


def batch_product(left, right):
    return jnp.einsum("pij,pjk->pik", left, right, precision=lax.Precision.HIGHEST)


def batch_apply(left, vector):
    return jnp.einsum("pij,pj->pi", left, vector, precision=lax.Precision.HIGHEST)


def analysis_weights(gram, drive_vec):
    members = gram.shape[1]
    identity = jnp.eye(members, dtype=jnp.float32)
    system = (members - 1.0) * identity + gram
    frobenius = jnp.sqrt(jnp.sum(system * system, axis=(1, 2)))
    scaled_sys = system / frobenius[:, None, None]
    inverse_root = jnp.broadcast_to(identity, system.shape)
    for sweep_index in range(ITERS):
        correction = 1.5 * identity - 0.5 * batch_product(inverse_root, scaled_sys)
        scaled_sys = batch_product(scaled_sys, correction)
        inverse_root = batch_product(correction, inverse_root)
    root = inverse_root / jnp.sqrt(frobenius)[:, None, None]
    mean_weight = batch_apply(root, batch_apply(root, drive_vec))
    return (jnp.sqrt(members - 1.0) * root + mean_weight[:, :, None]).astype(jnp.bfloat16)


def slot_positions(block_owner, devices, capacity):
    block_dest = block_owner[:, 0]
    onehot = (block_dest[:, None] == jnp.arange(devices, dtype=jnp.int32)[None, :]).astype(
        jnp.int32
    )
    position = jnp.sum(jnp.cumsum(onehot, axis=0) * onehot, axis=1) - 1
    return block_dest * capacity + position


def local(prior, obs_prior, obs_depart, obs_rinv, loc_class, block_owner, block_patch):
    mem_count = lax.axis_size("mem")
    patch_count = lax.axis_size("patch")
    devices = mem_count * patch_count
    member_part, lf_part, all_cols = prior.shape
    members = member_part * mem_count
    block_count, unused_members, obs_count = obs_prior.shape
    fields = lax.all_to_all(
        lax.all_to_all(prior, "mem", split_axis=2, concat_axis=0, tiled=True),
        "patch",
        split_axis=2,
        concat_axis=1,
        tiled=True,
    )
    col_part = fields.shape[-1]
    capacity = 2 * block_count // devices
    capacity_all = devices * capacity
    slot_index = slot_positions(block_owner, devices, capacity)
    send_patch = jnp.full((capacity_all,), -1, jnp.int32).at[slot_index].set(block_patch)
    send_values = (
        jnp.zeros((capacity_all, members, obs_count), jnp.bfloat16).at[slot_index].set(obs_prior)
    )
    send_depart = jnp.zeros((capacity_all, obs_count), jnp.bfloat16).at[slot_index].set(obs_depart)
    send_rinv = jnp.zeros((capacity_all, obs_count), jnp.bfloat16).at[slot_index].set(obs_rinv)
    send_class = jnp.zeros((capacity_all, obs_count), jnp.int32).at[slot_index].set(loc_class)
    arrived = (
        lax.all_to_all(send_values, ("mem", "patch"), split_axis=0, concat_axis=0, tiled=True),
        lax.all_to_all(send_depart, ("mem", "patch"), split_axis=0, concat_axis=0, tiled=True),
        lax.all_to_all(send_rinv, ("mem", "patch"), split_axis=0, concat_axis=0, tiled=True),
        lax.all_to_all(send_class, ("mem", "patch"), split_axis=0, concat_axis=0, tiled=True),
        lax.all_to_all(send_patch, ("mem", "patch"), split_axis=0, concat_axis=0, tiled=True),
    )
    gram_blocks, drive_vec = block_terms(arrived[0], arrived[1], arrived[2], arrived[3])
    select = (arrived[4][:, None] == jnp.arange(PD, dtype=jnp.int32)[None, :]).astype(jnp.float32)
    gram = jnp.einsum("sp,skj->pkj", select, gram_blocks, precision=lax.Precision.HIGHEST)
    drive_sum = jnp.einsum("sp,sk->pk", select, drive_vec, precision=lax.Precision.HIGHEST)
    weights = analysis_weights(gram, drive_sum)
    owner_patch = jnp.arange(col_part, dtype=jnp.int32) // (col_part // PD)
    average = jnp.sum(fields, axis=0, dtype=jnp.float32) / members
    deviation = (fields.astype(jnp.float32) - average).astype(jnp.bfloat16)
    mixed = jnp.zeros(fields.shape, jnp.float32)
    for patch_slot in range(PD):
        term = jnp.einsum(
            "kj,kfc->jfc", weights[patch_slot], deviation, preferred_element_type=jnp.float32
        )
        mixed = mixed + jnp.where(owner_patch == patch_slot, term, 0.0)
    analysis = (average + mixed).astype(jnp.bfloat16)
    widened = analysis.reshape(members, analysis.shape[1], 1, col_part)
    returned = lax.all_to_all(
        lax.all_to_all(widened, "mem", split_axis=0, concat_axis=2, tiled=True),
        "patch",
        split_axis=1,
        concat_axis=3,
        tiled=True,
    )
    result = returned.reshape(member_part, lf_part, all_cols)
    return result


def solution(mesh):
    return jax.shard_map(
        local,
        mesh=mesh,
        in_specs=(
            P("mem", "patch", None),
            P(("mem", "patch"), None, None),
            P(("mem", "patch"), None),
            P(("mem", "patch"), None),
            P(("mem", "patch"), None),
            P(("mem", "patch"), None),
            P(("mem", "patch")),
        ),
        out_specs=P("mem", "patch", None),
        check_vma=False,
    )
```

profile of v0, /device:TPU:0, one launch (start us, length us, event | category | flops | bytes accessed | tf_op | source)
XLA Modules:
  0.0 1025.2 jit_solution(17504251240305546727)
XLA Ops:
  0.9 0.8 select_reduce_fusion
  2.4 1.1 scatter_custom_fusion
  4.2 7.3 all-to-all-start.2
  11.5 1.7 scatter_custom_fusion.3
  13.2 5.4 all-to-all-done.2
  18.7 2.6 all-to-all-start.5
  21.2 1.8 scatter_custom_fusion.2
  23.0 5.6 all-to-all-done.5
  28.6 2.6 all-to-all-start.4
  31.2 39.3 %copy.133 = bf16[20,4,32768]{0,1,2:T(4,128)(2,1)} copy(bf16[20,4,32768]{2,1,0:T(4,128)(2,1)} %param.7) | data formatting | bytes 10485760 | tf_op args[0]
  70.5 107.3 %reshape.216 = bf16[4,2,327680]{2,1,0:T(2,128)(2,1)} reshape(bf16[32768,4,20]{2,1,0:T(4,128)(2,1)} %bitcast.246) | data formatting | bytes 10485760
  177.8 5.2 all-to-all-start
  183.0 3.0 broadcast_in_dim.111
  186.0 16.0 %scatter_fusion = bf16[256,80,128]{2,1,0:T(8,128)(2,1)} fusion(bf16[256,80,128]{2,1,0:T(8,128)(2,1)} %broadcast_in_dim.111, s32[128]{0:T(128)S(1)} %fusion.80, bf16[128,80,128]{2,1,0:T(8,128)(2,1)S(1)} %copy-done.1), kind=kCustom, calls=%fused_computation.1 | custom fusion | bytes 7864832 | tf_op jit(solution)/shard_map/scatter | solution.py:78
  202.0 40.2 %all-to-all-done = bf16[4,2,327680]{2,1,0:T(2,128)(2,1)} async-done(((bf16[4,2,327680]{2,1,0:T(2,128)(2,1)}), bf16[4,2,327680]{2,1,0:T(2,128)(2,1)}, u32[]{:S(2)}, u32[]{:S(2)}) %all-to-all-start) | async-done | bytes 5242912 | tf_op jit(solution)/shard_map/all_to_all | solution.py:66
  242.2 5.0 all-to-all-start.3
  247.3 1.7 scatter_custom_fusion.4
  255.6 105.1 %reshape.217 = bf16[32768,4,20]{2,1,0:T(4,128)(2,1)} reshape(bf16[4,2,327680]{2,1,0:T(2,128)(2,1)} %all-to-all-done) | data formatting | bytes 10485760
  360.7 43.5 %copy.134 = bf16[20,4,4,8192]{3,1,0,2:T(4,128)(2,1)} copy(bf16[20,4,4,8192]{0,1,3,2:T(4,128)(2,1)} %bitcast.245) | data formatting | bytes 10485760 | tf_op jit(solution)/shard_map/all_to_all | solution.py:66
  404.2 17.1 %copy.135 = bf16[80,4,8192]{0,1,2:T(4,128)(2,1)} copy(bf16[80,4,8192]{2,1,0:T(4,128)(2,1)} %bitcast.250) | data formatting | bytes 10485760 | tf_op jit(solution)/shard_map/all_to_all | solution.py:66
  421.3 5.9 all-to-all-start.6
  427.2 4.2 convert_reduce_fusion
  431.4 7.0 fusion.5
  438.5 7.6 multiply_reduce_fusion
  446.1 5.3 all-to-all-start.1
  451.4 5.3 fusion.4
  457.1 0.9 fusion.20
  458.7 0.9 fusion.24
  459.6 0.8 fusion.19
  462.0 0.8 fusion.18
  464.4 0.8 fusion.17
  465.9 1.2 fusion.87
  467.2 0.8 fusion.16
  478.2 1.0 fusion.98
  480.8 1.1 convolution_bitcast_fusion
  481.9 1.1 fusion.99
  483.3 151.8 %all-to-all-done.1 = bf16[80,4,8192]{0,1,2:T(4,128)(2,1)} async-done(((bf16[80,4,8192]{0,1,2:T(4,128)(2,1)}), bf16[80,4,8192]{0,1,2:T(4,128)(2,1)}, u32[]{:S(2)}, u32[]{:S(2)}) %all-to-all-start.1) | async-done | bytes 5242912 | tf_op jit(solution)/shard_map/all_to_all | solution.py:65
  635.1 12.9 %copy.136 = bf16[80,4,8192]{2,0,1:T(8,128)(2,1)} copy(bf16[80,4,8192]{0,1,2:T(4,128)(2,1)} %all-to-all-done.1) | data formatting | bytes 10485760 | tf_op jit(solution)/shard_map/all_to_all | solution.py:65
  648.0 7.7 convert_element_type.112
  655.8 13.7 %copy.200 = f32[40,8,8,1024]{3,2,1,0:T(8,128)S(1)} copy(f32[40,8,8,1024]{3,1,2,0:T(8,128)} %bitcast.249) | data formatting | bytes 20971520
  670.2 4.4 fusion.1
  674.7 5.4 copy.142
  680.1 5.7 fusion.41
  685.8 5.4 fusion.42
  691.2 5.5 fusion.43
  696.6 5.4 fusion.44
  702.0 5.5 fusion.45
  707.5 5.6 fusion.46
  713.1 5.5 fusion.47
  718.6 5.5 fusion.48
  724.1 5.5 fusion.49
  729.6 5.4 fusion.50
  735.0 5.5 fusion.51
  740.6 5.5 fusion.52
  746.0 5.4 fusion.53
  751.5 5.7 fusion.54
  757.3 5.5 fusion.55
  763.0 53.0 %fusion.8 = bf16[80,32,1,1024]{3,0,1,2:T(8,128)(2,1)} fusion(pred[1024]{0:T(1024)(128)(4,1)S(1)} %copy-done.16, f32[80,32,1024]{2,0,1:T(8,128)} %fusion.41, pred[1024]{0:T(1024)(128)(4,1)S(1)} %copy-done.17, f32[80,32,1024]{2,0,1:T(8,128)} %fusion.42, pred[1024]{0:T(1024)(128)(4,1)S(1)} %copy-done.14, f32[80,32,1024]{2,0,1:T(8,128)} %fusion.43, ...), kind=kOutput, calls=%fused_computation.19 | convolution fusion | flops 505937920 | bytes 167940096 | tf_op jit(solution)/shard_map/kj,kfc->jfc/dot_general | solution.py:100
  816.0 5.4 copy.159
  821.4 62.8 %all_to_all.104 = bf16[80,32,1,1024]{3,1,2,0:T(8,128)(2,1)S(1)} all-to-all(bf16[80,32,1,1024]{3,1,2,0:T(8,128)(2,1)S(1)} %copy.159), channel_id=1, replica_groups=mesh['mem'=4,'patch'=8] {'mem'}, dimensions={0} | all-to-all | bytes 10485760 | tf_op jit(solution)/shard_map/all_to_all | solution.py:107
  884.2 4.0 copy.160
  888.2 119.3 %all_to_all.105 = bf16[20,32,4,1024]{3,2,0,1:T(4,128)(2,1)S(1)} all-to-all(bf16[20,32,4,1024]{3,2,0,1:T(4,128)(2,1)S(1)} %copy.160), channel_id=1, replica_groups=mesh['mem'=4,'patch'=8] {'patch'}, dimensions={1} | all-to-all | bytes 10485760 | tf_op jit(solution)/shard_map/all_to_all | solution.py:106
  1007.5 7.9 copy.161
  1015.4 9.5 reshape.132
  (90 shorter events, 26.6 us)
Async XLA Ops:
  4.2 14.4 %all-to-all-start.2 = ((s32[32,8,1]{1,2,0:T(1,128)}), s32[32,8,1]{1,2,0:T(1,128)S(1)}, u32[]{:S(2)}, u32[]{:S(2)}) async-start(s32[32,8,1]{1,2,0:T(1,128)} %bitcast.7), calls=%async_computation.2 | async-start | bytes 32768 | tf_op jit(solution)/shard_map/all_to_all | solution.py:88
  18.7 10.0 all-to-all-start.5
  28.6 149.2 %all-to-all-start.4 = ((s32[32,8,128]{2,1,0:T(8,128)}), s32[32,8,128]{2,1,0:T(8,128)S(1)}, u32[]{:S(2)}, u32[]{:S(2)}) async-start(s32[32,8,128]{2,1,0:T(8,128)} %bitcast.9), calls=%async_computation.4 | async-start | bytes 262144 | tf_op jit(solution)/shard_map/all_to_all | solution.py:87
  177.8 8.2 copy-start.1
  177.8 64.4 %all-to-all-start = ((bf16[4,2,327680]{2,1,0:T(2,128)(2,1)}), bf16[4,2,327680]{2,1,0:T(2,128)(2,1)}, u32[]{:S(2)}, u32[]{:S(2)}) async-start(bf16[4,2,327680]{2,1,0:T(2,128)(2,1)} %reshape.216), calls=%async_computation | async-start | bytes 10485760 | tf_op jit(solution)/shard_map/all_to_all | solution.py:66
  242.2 179.1 %all-to-all-start.3 = ((bf16[256,80,128]{2,1,0:T(8,128)(2,1)}), bf16[256,80,128]{2,1,0:T(8,128)(2,1)}, u32[]{:S(2)}, u32[]{:S(2)}) async-start(bf16[256,80,128]{2,1,0:T(8,128)(2,1)} %scatter_fusion), calls=%async_computation.3 | async-start | bytes 10485760 | tf_op jit(solution)/shard_map/all_to_all | solution.py:84
  421.3 24.7 %all-to-all-start.6 = ((bf16[32,8,128]{2,1,0:T(8,128)(2,1)}), bf16[32,8,128]{2,1,0:T(8,128)(2,1)}, u32[]{:S(2)}, u32[]{:S(2)}) async-start(bf16[32,8,128]{2,1,0:T(8,128)(2,1)} %bitcast.12), calls=%async_computation.6 | async-start | bytes 131072 | tf_op jit(solution)/shard_map/all_to_all | solution.py:85
  446.0 10.7 %copy-start.18 = (f32[16]{0:T(128)S(1)}, f32[16]{0:T(128)}, u32[]{:S(2)}) copy-start(f32[16]{0:T(128)} %get-tuple-element.7) | copy-start | bytes 196
  446.1 189.1 %all-to-all-start.1 = ((bf16[80,4,8192]{0,1,2:T(4,128)(2,1)}), bf16[80,4,8192]{0,1,2:T(4,128)(2,1)}, u32[]{:S(2)}, u32[]{:S(2)}) async-start(bf16[80,4,8192]{0,1,2:T(4,128)(2,1)} %copy.135), calls=%async_computation.1 | async-start | bytes 16777216 | tf_op jit(solution)/shard_map/all_to_all | solution.py:65
  680.1 77.1 %copy-start = (bf16[80,8,4,1024]{3,0,2,1:T(8,128)(2,1)}, bf16[80,8,4,1024]{3,0,2,1:T(8,128)(2,1)S(1)}, u32[]{:S(2)}) copy-start(bf16[80,8,4,1024]{3,0,2,1:T(8,128)(2,1)S(1)} %copy.142) | copy-start | bytes 15728644
  757.2 5.7 copy-start.2
  757.2 5.7 copy-start.3
  757.2 5.7 copy-start.4
  757.2 5.7 copy-start.5
  757.2 5.7 copy-start.6
  757.2 5.7 copy-start.7
  757.2 5.7 copy-start.8
  757.2 5.7 copy-start.9
  757.2 5.7 copy-start.10
  757.2 5.7 copy-start.11
  757.2 5.7 copy-start.12
  757.3 5.7 copy-start.13
  757.3 5.7 copy-start.14
  757.3 5.7 copy-start.15
  757.3 5.7 copy-start.16
  757.3 5.7 copy-start.17
where the time goes:
time: 1030 us
  local copies, waits for them, and re-layouts  398 us (39%)
  waiting for transfers between devices  203 us (20%)
  blocking collectives  182 us (18%)
  matrix products  181 us (18%)
  starting transfers between devices  33.9 us (3%)
  other arithmetic  25.8 us (3%)
    unnamed x42, local copies, waits for them, and re-layouts  266 us
    all_to_all x1, waiting for transfers between devices, local(): lax.all_to_all(lax.all_to_all(prior, 'mem', split_axis=2, concat_axis=0,...  152 us
    dot_general x16, matrix products, local(): jnp.einsum('kj,kfc->jfc', weights[patch_slot], deviation, preferred_eleme...  136 us
    all_to_all x1, blocking collectives, local(): lax.all_to_all(lax.all_to_all(widened, 'mem', split_axis=0, concat_axis=2...  119 us
    all_to_all x1, blocking collectives, local(): lax.all_to_all(widened, 'mem', split_axis=0, concat_axis=2, tiled=True)  62.8 us
    all_to_all x2, local copies, waits for them, and re-layouts, local(): lax.all_to_all(prior, 'mem', split_axis=2, concat_axis=0, tiled=True)  60.6 us
    all_to_all x1, waiting for transfers between devices, local(): lax.all_to_all(prior, 'mem', split_axis=2, concat_axis=0, tiled=True)  40.2 us
    dot_general x29, matrix products, batch_product(): jnp.einsum('pij,pjk->pik', left, right, precision=lax.Precision.HIGHEST)  23.5 us
  transfers between devices with their start and end apart: 7, of which 4 were waited for; matrix products, arithmetic and copies ran while one was open for 38% of the time, Pallas kernels for 0%

commit v1 on v0

v1 whole, which is shorter than its diff:
```python
import functools
import jax
import jax.numpy as jnp
from jax import lax
from jax.experimental import pallas as pl
from jax.experimental.pallas import tpu as pltpu
from jax.sharding import PartitionSpec as P

PD = 16
ITERS = 10
LANES = 128
CHUNK = 512
MESH = pl.DeviceIdType.MESH


def batch_product(left, right):
    return jnp.einsum("pij,pjk->pik", left, right, precision=lax.Precision.HIGHEST)


def batch_apply(left, vector):
    return jnp.einsum("pij,pj->pi", left, vector, precision=lax.Precision.HIGHEST)


def analysis_weights(gram, drive_vec):
    members = gram.shape[1]
    identity = jnp.eye(members, dtype=jnp.float32)
    system = (members - 1.0) * identity + gram
    frobenius = jnp.sqrt(jnp.sum(system * system, axis=(1, 2)))
    scaled_sys = system / frobenius[:, None, None]
    inverse_root = jnp.broadcast_to(identity, system.shape)
    for sweep_index in range(ITERS):
        correction = 1.5 * identity - 0.5 * batch_product(inverse_root, scaled_sys)
        scaled_sys = batch_product(scaled_sys, correction)
        inverse_root = batch_product(correction, inverse_root)
    root = inverse_root / jnp.sqrt(frobenius)[:, None, None]
    mean_weight = batch_apply(root, batch_apply(root, drive_vec))
    return (jnp.sqrt(members - 1.0) * root + mean_weight[:, :, None]).astype(jnp.bfloat16)


def slot_positions(block_owner, devices, capacity):
    block_dest = block_owner[:, 0]
    onehot = (block_dest[:, None] == jnp.arange(devices, dtype=jnp.int32)[None, :]).astype(
        jnp.int32
    )
    position = jnp.sum(jnp.cumsum(onehot, axis=0) * onehot, axis=1) - 1
    return block_dest * capacity + position


def spread_kernel(index, blocks, slots, sem):
    count = blocks.shape[0]

    def copy(b):
        return pltpu.make_async_copy(blocks.at[b], slots.at[index[b]], sem.at[b])

    def start(b, carry):
        copy(b).start()
        return carry

    def finish(b, carry):
        copy(b).wait()
        return carry

    lax.fori_loop(0, count, start, 0)
    lax.fori_loop(0, count, finish, 0)


def spread_blocks(index, blocks, total):
    return pl.pallas_call(
        spread_kernel,
        out_shape=jax.ShapeDtypeStruct((total,) + blocks.shape[1:], blocks.dtype),
        in_specs=[pl.BlockSpec(memory_space=pltpu.SMEM), pl.BlockSpec(memory_space=pl.ANY)],
        out_specs=pl.BlockSpec(memory_space=pl.ANY),
        scratch_shapes=[pltpu.SemaphoreType.DMA((blocks.shape[0],))],
        name="spread_blocks",
    )(index, blocks)


def exchange_kernel(mems, patches, prior, slots, aux, fields, got_slots, got_aux,
                    slot_send, slot_recv, aux_send, aux_recv, col_send, col_recv, own_sem):
    my_mem, my_patch = lax.axis_index("mem"), lax.axis_index("patch")
    devices = mems * patches
    me = my_mem * patches + my_patch
    cols = fields.shape[-1]

    def partner(step):
        dest = lax.rem(me + step, devices)
        return dest, (dest // patches, lax.rem(dest, patches))

    barrier = pltpu.get_barrier_semaphore()

    def greet(step, carry):
        pl.semaphore_signal(barrier, inc=1, device_id=partner(step)[1], device_id_type=MESH)
        return carry

    lax.fori_loop(1, devices, greet, 0)
    pl.semaphore_wait(barrier, devices - 1)

    def slot_copies(step):
        dest, where = partner(step)
        return (
            pltpu.make_async_remote_copy(
                src_ref=slots.at[dest], dst_ref=got_slots.at[me],
                send_sem=slot_send.at[step], recv_sem=slot_recv.at[step],
                device_id=where, device_id_type=MESH),
            pltpu.make_async_remote_copy(
                src_ref=aux.at[dest], dst_ref=got_aux.at[me],
                send_sem=aux_send.at[step], recv_sem=aux_recv.at[step],
                device_id=where, device_id_type=MESH),
        )

    def col_copy(step):
        dest = lax.rem(my_mem + step, mems)
        first = pl.multiple_of(dest * cols, LANES)
        return pltpu.make_async_remote_copy(
            src_ref=prior.at[:, :, pl.ds(first, cols)], dst_ref=fields.at[my_mem],
            send_sem=col_send.at[step], recv_sem=col_recv.at[step],
            device_id=(dest, my_patch), device_id_type=MESH)

    def start(step, carry):
        for copy in slot_copies(step):
            copy.start()
        return carry

    def finish(step, carry):
        for copy in slot_copies(step):
            copy.wait()
        return carry

    lax.fori_loop(1, devices, start, 0)
    for step in range(1, mems):
        col_copy(step).start()
    mine = (
        pltpu.make_async_copy(slots.at[me], got_slots.at[me], own_sem.at[0]),
        pltpu.make_async_copy(aux.at[me], got_aux.at[me], own_sem.at[1]),
        pltpu.make_async_copy(
            prior.at[:, :, pl.ds(pl.multiple_of(my_mem * cols, LANES), cols)],
            fields.at[my_mem], own_sem.at[2]),
    )
    for copy in mine:
        copy.start()
    for copy in mine:
        copy.wait()
    lax.fori_loop(1, devices, finish, 0)
    for step in range(1, mems):
        col_copy(step).wait()


def exchange(prior, slots, aux, mems, patches):
    part, lf, all_cols = prior.shape
    devices = mems * patches
    dma = pltpu.SemaphoreType.DMA
    return pl.pallas_call(
        functools.partial(exchange_kernel, mems, patches),
        out_shape=(
            jax.ShapeDtypeStruct((mems, part, lf, all_cols // mems), jnp.bfloat16),
            jax.ShapeDtypeStruct(slots.shape, slots.dtype),
            jax.ShapeDtypeStruct(aux.shape, aux.dtype),
        ),
        in_specs=[pl.BlockSpec(memory_space=pl.ANY)] * 3,
        out_specs=(pl.BlockSpec(memory_space=pl.ANY),) * 3,
        scratch_shapes=[dma((devices,)), dma((devices,)), dma((devices,)), dma((devices,)),
                        dma((mems,)), dma((mems,)), dma((3,))],
        compiler_params=pltpu.CompilerParams(collective_id=0, has_side_effects=True),
        name="exchange",
    )(prior, slots, aux)


def apply_kernel(mems, chunks, fields, weights, out, wide, mixed, buf, send, recv, own):
    my_mem, my_patch = lax.axis_index("mem"), lax.axis_index("patch")
    step = pl.program_id(0)
    part, lf, chunk = fields.shape[1], fields.shape[2], fields.shape[3]
    members = mems * part
    tiles = chunk // LANES
    cols = chunk * chunks
    half = LANES // 2

    @pl.when(step == 0)
    def _():
        barrier = pltpu.get_barrier_semaphore()
        for other in range(1, mems):
            pl.semaphore_signal(barrier, inc=1,
                                device_id=(lax.rem(my_mem + other, mems), my_patch),
                                device_id_type=MESH)
        pl.semaphore_wait(barrier, mems - 1)

    def place(owner, at):
        return out.at[:, :, pl.ds(pl.multiple_of(owner * cols + at * chunk, LANES), chunk)]

    def outgoing(at, other):
        dest = lax.rem(my_mem + other, mems)
        return pltpu.make_async_remote_copy(
            src_ref=buf.at[lax.rem(at, 2), dest], dst_ref=place(my_mem, at),
            send_sem=send.at[lax.rem(at, 2), other], recv_sem=recv.at[at, other],
            device_id=(dest, my_patch), device_id_type=MESH)

    def local_copy(at):
        return pltpu.make_async_copy(buf.at[lax.rem(at, 2), my_mem], place(my_mem, at),
                                     own.at[lax.rem(at, 2)])

    def drain(at):
        for other in range(1, mems):
            outgoing(at, other).wait_send()
        local_copy(at).wait()

    @pl.when(step >= 2)
    def _():
        drain(step - 2)

    for k in range(members):
        row = fields[k // part, k % part].astype(jnp.float32)
        for t in range(tiles):
            wide[t, lf * k:lf * k + lf, :] = row[:, t * LANES:(t + 1) * LANES]
    lane = lax.broadcasted_iota(jnp.int32, (members, LANES), 1)
    for t in range(tiles):
        averages, devs = [], []
        for f in range(lf):
            x = wide[t, pl.ds(f, members, stride=lf), :]
            average = jnp.sum(x, axis=0, keepdims=True) / members
            averages.append(average)
            devs.append((x - average).astype(jnp.bfloat16))
        y = jnp.dot(weights[t], jnp.concatenate(devs, axis=1), preferred_element_type=jnp.float32)
        for f in range(lf):
            z = y[:, f * LANES:(f + 1) * LANES]
            mixed[t, pl.ds(f, members, stride=lf), :] = averages[f] + jnp.where(
                lane < half, z[:members], z[members:])
    slot = lax.rem(step, 2)
    for j in range(members):
        row = jnp.concatenate([mixed[t, lf * j:lf * j + lf, :] for t in range(tiles)], axis=1)
        buf[slot, j // part, j % part] = row.astype(jnp.bfloat16)
    for other in range(1, mems):
        outgoing(step, other).start()
    local_copy(step).start()

    @pl.when(step == chunks - 1)
    def _():
        if chunks > 1:
            drain(step - 1)
        drain(step)

        def arrive(at, carry):
            for other in range(1, mems):
                outgoing(at, other).wait_recv()
            return carry

        lax.fori_loop(0, chunks, arrive, 0)


def apply_return(fields, weights, mems):
    unused, part, lf, cols = fields.shape
    members = mems * part
    chunk = CHUNK
    chunks = cols // chunk
    tiles = chunk // LANES
    dma = pltpu.SemaphoreType.DMA
    return pl.pallas_call(
        functools.partial(apply_kernel, mems, chunks),
        grid=(chunks,),
        out_shape=jax.ShapeDtypeStruct((part, lf, cols * mems), jnp.bfloat16),
        in_specs=[
            pl.BlockSpec((mems, part, lf, chunk), lambda i: (0, 0, 0, i)),
            pl.BlockSpec((tiles, 2 * members, members), lambda i: (i, 0, 0)),
        ],
        out_specs=pl.BlockSpec(memory_space=pl.ANY),
        scratch_shapes=[
            pltpu.VMEM((tiles, members * lf, LANES), jnp.float32),
            pltpu.VMEM((tiles, members * lf, LANES), jnp.float32),
            pltpu.VMEM((2, mems, part, lf, chunk), jnp.bfloat16),
            dma((2, mems)), dma((chunks, mems)), dma((2,)),
        ],
        compiler_params=pltpu.CompilerParams(collective_id=1, has_side_effects=True,
                                             vmem_limit_bytes=32 * 1024 * 1024),
        name="apply_return",
    )(fields, weights)


def local(prior, obs_prior, obs_depart, obs_rinv, loc_class, block_owner, block_patch):
    mems = lax.axis_size("mem")
    patches = lax.axis_size("patch")
    devices = mems * patches
    block_count, members, obs_count = obs_prior.shape
    capacity = 2 * block_count // devices
    slot_index = slot_positions(block_owner, devices, capacity)
    total = devices * capacity
    taper = 1.0 - loc_class.astype(jnp.float32) * 0.0625
    taper = (taper * taper).astype(jnp.bfloat16)
    tag = jnp.broadcast_to((block_patch + 1).astype(jnp.bfloat16)[:, None], obs_depart.shape)
    packed = jnp.stack([obs_depart, obs_rinv, taper, tag], axis=1)
    place = (slot_index[None, :] == jnp.arange(total, dtype=jnp.int32)[:, None])
    aux = jnp.einsum("sb,bro->sro", place.astype(jnp.bfloat16), packed,
                     preferred_element_type=jnp.float32).astype(jnp.bfloat16)
    slots = spread_blocks(slot_index, obs_prior, total)
    fields, got_slots, got_aux = exchange(
        prior,
        slots.reshape(devices, capacity, members, obs_count),
        aux.reshape(devices, capacity, 4, obs_count),
        mems, patches)
    side = got_aux.reshape(total, 4, obs_count)
    values = got_slots.reshape(total, members, obs_count)
    values = jnp.where(side[:, 3:4, :] > 0, values, jnp.zeros((), jnp.bfloat16))
    depart = side[:, 0]
    factor = side[:, 1].astype(jnp.float32) * side[:, 2].astype(jnp.float32)
    patch_of = side[:, 3, 0].astype(jnp.float32)
    average = jnp.sum(values, axis=1, keepdims=True, dtype=jnp.float32) / members
    deviation = (values.astype(jnp.float32) - average).astype(jnp.bfloat16)
    scaled = (deviation.astype(jnp.float32) * factor[:, None, :]).astype(jnp.bfloat16)
    gram_blocks = jnp.einsum("bko,bjo->bkj", scaled, deviation, preferred_element_type=jnp.float32)
    drive_blocks = jnp.einsum("bko,bo->bk", scaled, depart, preferred_element_type=jnp.float32)
    select = (patch_of[:, None] == (jnp.arange(PD, dtype=jnp.float32) + 1.0)[None, :]).astype(
        jnp.float32)
    gram = jnp.einsum("sp,skj->pkj", select, gram_blocks, precision=lax.Precision.HIGHEST)
    drive = jnp.einsum("sp,sk->pk", select, drive_blocks, precision=lax.Precision.HIGHEST)
    weights = jnp.swapaxes(analysis_weights(gram, drive), 1, 2)
    gathered = lax.all_gather(weights, "patch", axis=0, tiled=True)
    gathered = gathered.reshape(patches * PD // 2, 2 * members, members)
    return apply_return(fields, gathered, mems)


def solution(mesh):
    return jax.shard_map(
        local,
        mesh=mesh,
        in_specs=(
            P("mem", "patch", None),
            P(("mem", "patch"), None, None),
            P(("mem", "patch"), None),
            P(("mem", "patch"), None),
            P(("mem", "patch"), None),
            P(("mem", "patch"), None),
            P(("mem", "patch")),
        ),
        out_specs=P("mem", "patch", None),
        check_vma=False,
    )
```

time: 1030 us -> 413 us (0.40)
  local copies, waits for them, and re-layouts: 398 us -> 11 us
  Pallas kernels: 0 us -> 278 us
  blocking collectives: 182 us -> 0 us
  waiting for transfers between devices: 203 us -> 42.8 us
  matrix products: 181 us -> 45.4 us
  starting transfers between devices: 33.9 us -> 0.01 us
  between operations: 0.97 us -> 14.2 us
  other arithmetic: 25.8 us -> 14.3 us
    pallas_call x0 -> x3, Pallas kernels: none -> 278 us  [the longest x1 134 us: exchange(): pl.pallas_call(functools.partial(exchange_kernel, mems, patches), out_sha...]
    unnamed x42 -> x11, local copies, waits for them, and re-layouts: 266 us -> 6.7 us
    all_to_all x7 -> x0, waiting for transfers between devices: 203 us -> none  [the longest x1 152 us: local(): lax.all_to_all(lax.all_to_all(prior, 'mem', split_axis=2, concat_axis=0,...]
    all_to_all x2 -> x0, blocking collectives: 182 us -> none  [the longest x1 119 us: local(): lax.all_to_all(lax.all_to_all(widened, 'mem', split_axis=0, concat_axis=2...]
    dot_general x19 -> x4, matrix products: 148 us -> 9.71 us  [the longest x1 5.68 us: local(): jnp.einsum('bko,bjo->bkj', scaled, deviation, preferred_element_type=jnp....]
    all_to_all x7 -> x0, local copies, waits for them, and re-layouts: 86.7 us -> none  [the longest x2 60.6 us: local(): lax.all_to_all(prior, 'mem', split_axis=2, concat_axis=0, tiled=True)]
    all_gather x0 -> x1, waiting for transfers between devices: none -> 42.8 us  [local(): gathered = lax.all_gather(weights, 'patch', axis=0, tiled=True)]
    all_to_all x7 -> x0, starting transfers between devices: 33.9 us -> none  [the longest x1 7.3 us: local(): lax.all_to_all(send_patch, ('mem', 'patch'), split_axis=0, concat_axis=0,...]
  transfers between devices with their start and end apart: 7 -> 1, of which waited for: 4 -> 1; matrix products, arithmetic and copies ran while one was open for 38% -> 0% of each run, Pallas kernels for 0% -> 0%
where the time goes in v1:
time: 413 us; the launch traced here: 406 us
  Pallas kernels  278 us (67%)
  matrix products  45.4 us (11%)
  waiting for transfers between devices  42.8 us (10%)
  other arithmetic  14.3 us (3%)
  between operations  14.2 us (3%)
  local copies, waits for them, and re-layouts  11 us (3%)
    pallas_call x1, Pallas kernels, exchange(): pl.pallas_call(functools.partial(exchange_kernel, mems, patches), out_sha...  134 us
    pallas_call x1, Pallas kernels, spread_blocks(): pl.pallas_call(spread_kernel, out_shape=jax.ShapeDtypeStruct((total,) + b...  82.3 us
    pallas_call x1, Pallas kernels, apply_return(): pl.pallas_call(functools.partial(apply_kernel, mems, chunks), grid=(chunk...  61.3 us
    all_gather x1, waiting for transfers between devices, local(): gathered = lax.all_gather(weights, 'patch', axis=0, tiled=True)  42.8 us
    dot_general x29, matrix products, batch_product(): jnp.einsum('pij,pjk->pik', left, right, precision=lax.Precision.HIGHEST)  23.4 us
    dot_general x1, matrix products, local(): jnp.einsum('sp,skj->pkj', select, gram_blocks, precision=lax.Precision.HI...  10.1 us
  transfers between devices with their start and end apart: 1, of which 1 were waited for; matrix products, arithmetic and copies ran while one was open for 0% of the time, Pallas kernels for 0%

profile of v1, /device:TPU:0, one launch (start us, length us, event | category | flops | bytes accessed | tf_op | source)
XLA Modules:
  0.0 405.6 jit_solution(8406503800654407728)
XLA Ops:
  6.5 0.0 all-gather.2.cloned.1.call-start
  6.6 0.7 add_convert_fusion.1
  7.2 0.9 fusion.42
  8.1 0.7 fusion.38
  8.8 0.2 reduce_window_sum.11
  9.0 0.8 select_reduce_fusion
  9.9 0.7 add_add_fusion.index
  10.5 0.1 stack_broadcast_in_dim.2
  10.6 1.0 convolution_convert_fusion
  11.6 0.9 copy.19
  12.5 0.0 copy-done.3
  12.5 82.3 %spread_blocks.1 = bf16[256,80,128]{2,1,0:T(8,128)(2,1)} custom-call(s32[128]{0:T(128)} %copy-done.3, bf16[128,80,128]{2,1,0:T(8,128)(2,1)} %blocks.1), custom_call_target="tpu_custom_call" | custom-call | tf_op jit(solution)/shard_map/spread_blocks/pallas_call | solution.py:68
  94.9 134.4 %exchange.1 = (bf16[4,20,4,8192]{3,2,1,0:T(4,128)(2,1)}, bf16[32,8,80,128]{3,2,1,0:T(8,128)(2,1)}, bf16[32,8,4,128]{3,2,1,0:T(4,128)(2,1)}) custom-call(bf16[20,4,32768]{2,1,0:T(4,128)(2,1)} %prior.1, bf16[32,8,80,128]{3,2,1,0:T(8,128)(2,1)} %bitcast.110, bf16[32,8,4,128]{3,2,1,0:T(4,128)(2,1)} %bitcast.114), custom_call_target="tpu_custom_call" | custom-call | tf_op jit(solution)/shard_map/exchange/pallas_call | solution.py:152
  229.2 1.1 slice.20
  230.3 1.3 fusion.26
  231.6 1.3 fusion.50
  233.0 0.1 copy.33
  233.1 5.6 %convert_reduce_fusion = f32[32,8,128]{2,1,0:T(8,128)S(1)} fusion(bf16[32,8,80,128]{3,2,1,0:T(8,128)(2,1)} %get-tuple-element.10, pred[32,8,128]{2,1,0:T(8,128)(4,1)S(1)} %fusion.129), kind=kLoop, calls=%fused_computation.4 | loop fusion | flops 7831552 | bytes 5406720 | tf_op jit(solution)/shard_map/reduce_sum | solution.py:303
  238.7 0.0 copy-done.2
  238.7 3.1 subtract_convert_fusion
  241.8 5.7 %fusion.3 = f32[256,80,80]{2,1,0:T(8,128)} fusion(bf16[256,80,128]{2,1,0:T(8,128)(2,1)S(1)} %subtract_convert_fusion, f32[256,128]{1,0:T(8,128)S(1)} %bitcast.115), kind=kOutput, calls=%fused_computation.6 | convolution fusion | flops 427294720 | bytes 11927552 | tf_op jit(solution)/shard_map/bko,bjo->bkj/dot_general | solution.py:306
  247.5 10.1 %multiply_reduce_fusion = (f32[16]{0:T(128)S(1)}, f32[16,80,80]{2,0,1:T(8,128)S(1)}) fusion(f32[256,80,80]{2,1,0:T(8,128)} %fusion.3, f32[256]{0:T(256)S(1)} %bitcast.121, f32[16]{0:T(128)S(1)} %iota_add_fusion, f32[80,80]{1,0:T(8,128)S(1)} %fusion.39), kind=kOutput, calls=%fused_computation.35 | convolution fusion | flops 314884096 | bytes 6989952 | tf_op jit(solution)/shard_map/sp,skj->pkj/dot_general | solution.py:310
  257.5 0.1 broadcast_divide_fusion
  257.7 0.9 fusion.15
  258.6 0.9 fusion.19
  259.5 0.7 fusion.23
  260.2 0.8 fusion.14
  261.0 0.8 fusion.52
  261.8 0.8 fusion.51
  262.6 1.0 fusion.13
  263.6 0.8 fusion.54
  264.4 0.8 fusion.53
  265.2 0.8 fusion.12
  266.0 0.8 fusion.56
  266.8 0.8 fusion.55
  267.6 0.8 fusion.11
  268.4 0.8 fusion.58
  269.1 0.8 fusion.57
  269.9 0.8 fusion.10
  270.7 0.8 fusion.60
  271.5 0.8 fusion.59
  272.3 0.8 fusion.9
  273.1 0.8 fusion.62
  273.9 0.8 fusion.61
  274.7 1.1 fusion.8
  275.7 0.8 fusion.64
  276.5 0.8 fusion.63
  277.3 0.8 fusion.7
  278.1 0.8 fusion.65
  278.9 0.8 fusion.66
  279.7 2.8 fusion.2
  282.5 0.2 fusion.43
  282.7 0.8 fusion.6
  283.5 0.8 convolution_divide_fusion
  284.3 1.1 convolution_bitcast_fusion
  285.4 1.1 fusion.67
  286.6 0.2 fusion.22
  286.8 0.9 copy.26
  287.7 0.0 all-gather.2.cloned.1.call-update
  287.7 42.8 %all-gather.2.cloned.1.call-done = bf16[128,80,80]{2,1,0:T(8,128)(2,1)} async-done(((bf16[16,80,80]{2,1,0:T(8,128)(2,1)}), bf16[128,80,80]{2,1,0:T(8,128)(2,1)}) %all-gather.2.cloned.1.call-update) | async-done | bytes 1638416 | tf_op jit(solution)/shard_map/all_gather | solution.py:313
  330.5 2.5 copy-done
  333.0 1.7 copy-done.1
  334.7 61.3 %apply_return.1 = bf16[20,4,32768]{2,1,0:T(4,128)(2,1)S(1)} custom-call(bf16[4,20,4,8192]{3,2,1,0:T(4,128)(2,1)S(1)} %copy-done, bf16[64,160,80]{2,1,0:T(8,128)(2,1)S(1)} %bitcast.109), custom_call_target="tpu_custom_call" | custom-call | tf_op jit(solution)/shard_map/apply_return/pallas_call | solution.py:255
  396.0 2.4 copy.56
  (14 shorter events, 0.1 us)
Async XLA Ops:
  6.5 324.0 %all-gather.2.cloned.1.call-start = ((), (), s32[]{:S(2)}) async-start(), calls=%async_computation | async-start | bytes 2949120 | tf_op jit(solution)/shard_map/all_gather | solution.py:313
  10.5 2.0 copy-start.3
  233.1 5.6 %copy-start.2 = (bf16[32,8,80,128]{3,2,1,0:T(8,128)(2,1)S(1)}, bf16[32,8,80,128]{3,2,1,0:T(8,128)(2,1)}, u32[]{:S(2)}) copy-start(bf16[32,8,80,128]{3,2,1,0:T(8,128)(2,1)} %get-tuple-element.10) | copy-start | bytes 15728644
  330.5 2.5 copy-start
  333.0 1.7 copy-start.1
Sparse Core Ops, SparseCore 0:
  287.8 42.6 all-gather.1
